TPU v7x, 256 devices: a whole 4x4x8 slice. The times are simulated.
256 devices in a mesh: ctx: 64 (over y_hi, x, z), head: 4 (over y_lo, core).
Axes of the slice: x: 4, y: 4 (y_hi: 2, y_lo: 2; y = y_hi * 2 + y_lo), z: 8, core: 2. Of those that a mesh axis runs over, the one named last changes fastest.
Arguments:
- queries: bfloat16 [32768, 8192], P('ctx', 'head'), may hold values from -80 to 80
- keys: bfloat16 [32768, 1024], P(('ctx', 'head')), may hold values from -4 to 4
- values: bfloat16 [32768, 1024], P(('ctx', 'head')), may hold values from -6 to 6
- lengths: int32 [64], replicated, may hold values from 1 to 1024, 32768 in all
Outputs:
- attended: bfloat16 [32768, 8192], P('ctx', 'head')
Inputs may be any that keep to these rules, and one draw needn't show every extreme that they name: lengths sum to 32768; each document has 1 to 1024 tokens and one has exactly 1024.
All inputs are finite; a program needn't handle non-finite values.
Results may differ from a plain program's by a relative error of at most 0.0036.
Values may be sent and summed in bfloat16 or wider, within the bound.
A program may use at most 64 MiB of HBM per device.

v0:
```python
import jax
import jax.numpy as jnp
from jax import lax
from jax.sharding import PartitionSpec as P

HD = 128
REACH = 2


def passed_along(value, axis, steps):
    count = lax.axis_size(axis)
    leading, last = (max(0, -steps), min(count, count - steps))
    return lax.ppermute(value, axis, [(source, source + steps) for source in range(leading, last)])


def document_of(positions, doc_ends):
    counted = jnp.sum((positions[:, None] >= doc_ends[None, :]).astype(jnp.int32), axis=1)
    return jnp.where(positions < 0, -1, counted)


def per_device(queries, keys, values, lengths):
    stacked = jnp.stack([keys, values])
    received = lax.all_to_all(stacked, "head", split_axis=2, concat_axis=1, tiled=True)
    tok_rows = received.shape[1]
    earlier_blocks = []
    carried = received
    for step in range(REACH):
        carried = passed_along(carried, "ctx", 1)
        earlier_blocks = [carried] + earlier_blocks
    window = jnp.concatenate(earlier_blocks + [received], axis=1)
    key_width = window.shape[1]
    ctx_index = lax.axis_index("ctx")
    doc_ends = jnp.cumsum(lengths)
    query_pos = ctx_index * tok_rows + jnp.arange(tok_rows, dtype=jnp.int32)
    key_pos = (ctx_index - REACH) * tok_rows + jnp.arange(key_width, dtype=jnp.int32)
    allowed = (
        document_of(query_pos, doc_ends)[:, None] == document_of(key_pos, doc_ends)[None, :]
    ) & (key_pos[None, :] <= query_pos[:, None])
    query_heads = queries.shape[1] // HD
    group = query_heads // (window.shape[2] // HD)
    scale = HD ** (-0.5)

    def one_head(head, output):
        query_head = lax.dynamic_slice_in_dim(queries, head * HD, HD, 1)
        shared = head // group * HD
        key_head = lax.dynamic_slice_in_dim(window[0], shared, HD, 1)
        value_head = lax.dynamic_slice_in_dim(window[1], shared, HD, 1)
        scores = (
            lax.dot_general(
                query_head, key_head, (((1,), (1,)), ((), ())), preferred_element_type=jnp.float32
            )
            * scale
        )
        scores = jnp.where(allowed, scores, -jnp.inf)
        top = jnp.max(scores, axis=1, keepdims=True)
        weights = jnp.where(allowed, jnp.exp(scores - top), 0.0)
        total = jnp.sum(weights, axis=1, keepdims=True)
        rounded = weights.astype(jnp.bfloat16)
        mixed = jnp.dot(rounded, value_head, preferred_element_type=jnp.float32) / total
        return lax.dynamic_update_slice_in_dim(output, mixed.astype(jnp.bfloat16), head * HD, 1)

    return lax.fori_loop(0, query_heads, one_head, jnp.zeros(queries.shape, jnp.bfloat16))


def solution(mesh):
    placed = (P("ctx", "head"), P(("ctx", "head"), None), P(("ctx", "head"), None), P())
    return jax.shard_map(
        per_device, mesh=mesh, in_specs=placed, out_specs=P("ctx", "head"), check_vma=False
    )
```

profile of v0, /device:TPU:16, one launch (start us, length us, event | category | flops | bytes accessed | tf_op | source)
XLA Modules:
  0.0 135.1 jit_solution(2969903649965470095)
XLA Ops:
  0.0 1.1 pad_maximum_fusion.1
  1.5 11.2 %all_to_all.18 = bf16[2,128,1024]{1,0,2:T(2,128)(2,1)S(1)} all-to-all(bf16[2,128,1024]{1,0,2:T(2,128)(2,1)S(1)} %copy.16), channel_id=1, replica_groups=mesh['ctx'=64,'head'=4] {'head'}, dimensions={2} | all-to-all | bytes 1048576 | tf_op jit(solution)/shard_map/all_to_all | solution.py:23
  13.2 3.8 %collective-permute-start = (bf16[2,512,256]{2,1,0:T(8,128)(2,1)S(1)}, bf16[2,512,256]{2,1,0:T(8,128)(2,1)S(1)}, u32[]{:S(2)}, u32[]{:S(2)}) collective-permute-start(bf16[2,512,256]{2,1,0:T(8,128)(2,1)S(1)} %bitcast.20), channel_id=1, source_target_pairs={{0,4},{4,8},{8,12},{12,16},{16,20},{20,24},{24,28},{28,32},{32,36}... | collective-permute-start | bytes 1572872 | tf_op jit(solution)/shard_map/ppermute | solution.py:13
  17.5 17.2 %collective-permute-done = bf16[2,512,256]{2,1,0:T(8,128)(2,1)S(1)} collective-permute-done((bf16[2,512,256]{2,1,0:T(8,128)(2,1)S(1)}, bf16[2,512,256]{2,1,0:T(8,128)(2,1)S(1)}, u32[]{:S(2)}, u32[]{:S(2)}) %collective-permute-start) | collective-permute-done | bytes 524320 | tf_op jit(solution)/shard_map/ppermute | solution.py:13
  34.7 1.9 %collective-permute-start.1 = (bf16[2,512,256]{2,1,0:T(8,128)(2,1)S(1)}, bf16[2,512,256]{2,1,0:T(8,128)(2,1)S(1)}, u32[]{:S(2)}, u32[]{:S(2)}) collective-permute-start(bf16[2,512,256]{2,1,0:T(8,128)(2,1)S(1)} %collective-permute-done), channel_id=1, source_target_pairs={{0,4},{4,8},{8,12},{12,16},{16,20},{20,24},{24,28},{28,32},{32,36}... | collective-permute-start | bytes 1572872 | tf_op jit(solution)/shard_map/ppermute | solution.py:13
  36.7 18.3 %collective-permute-done.1 = bf16[2,512,256]{2,1,0:T(8,128)(2,1)S(1)} collective-permute-done((bf16[2,512,256]{2,1,0:T(8,128)(2,1)S(1)}, bf16[2,512,256]{2,1,0:T(8,128)(2,1)S(1)}, u32[]{:S(2)}, u32[]{:S(2)}) %collective-permute-start.1) | collective-permute-done | bytes 524320 | tf_op jit(solution)/shard_map/ppermute | solution.py:13
  55.1 1.6 %broadcast_in_dim.46 = bf16[512,2048]{1,0:T(8,128)(2,1)} broadcast(bf16[]{:T(256)} %constant.141.clone.1), dimensions={} | broadcast | bytes 2097154 | tf_op jit(solution)/shard_map/broadcast_in_dim | solution.py:62
  56.7 78.4 %while.16 = (s32[]{:T(128)}, bf16[512,2048]{1,0:T(8,128)(2,1)}, bf16[512,2048]{1,0:T(8,128)(2,1)}, bf16[2,1536,256]{2,1,0:T(8,128)(2,1)S(1)}, s32[1536]{0:T(1024...) while((s32[]{:T(128)}, bf16[512,2048]{1,0:T(8,128)(2,1)}, ...), condition=%wide.region_6.7_spmd.clone, body=%wide.region_3.6_spmd.clone.sunk | while | flops 416939008 | bytes 13699415 | solution.py:62
  56.8 1.8 %fusion.35 = (f32[512]{0:T(512)S(1)}, f32[512,1536]{1,0:T(8,128)S(1)}) fusion(bf16[1,1536,256]{2,1,0:T(8,128)(2,1)S(1)} %get-tuple-element.234, s32[]{:T(128)S(6)} %select_n.102, bf16[512,2048]{1,0:T(8,128)(2,1)} %get-tuple-element.272, s32[]{:T(128)S(6)} %select_n.100, s32[512]{0:T(512)S(1)} %get-tuple-element.276, ...), kind=kOutput, calls=%fused_computation.28.clone.1 | convolution fusion | flops 206044672 | bytes 3692552 | tf_op jit(solution)/shard_map/while/body/eval_jaxpr/dot_general | solution.py:49
  58.6 1.0 fusion.36
  59.6 2.0 %fusion.37 = bf16[512,2048]{1,0:T(8,128)(2,1)} fusion(bf16[512,2048]{1,0:T(8,128)(2,1)} %get-tuple-element.255, s32[]{:T(128)S(6)} %select_n.100, f32[512,1536]{1,0:T(8,128)S(1)} %get-tuple-element.235, s32[1536]{0:T(1024)S(1)} %get-tuple-element.277, s32[1536]{0:T(1024)S(1)} %get-tuple-element.274, f32[512]{0:T(512)S(1)} %get-tuple-element.236, ...), kind=kOutput, calls=%fused_computation.10.clone.1 | convolution fusion | flops 206176256 | bytes 3694600 | tf_op jit(solution)/shard_map/while/body/eval_jaxpr/dot_general | solution.py:59
  61.7 1.8 %fusion.35 = (f32[512]{0:T(512)S(1)}, f32[512,1536]{1,0:T(8,128)S(1)}) fusion(bf16[1,1536,256]{2,1,0:T(8,128)(2,1)S(1)} %get-tuple-element.234, s32[]{:T(128)S(6)} %select_n.102, bf16[512,2048]{1,0:T(8,128)(2,1)} %get-tuple-element.272, s32[]{:T(128)S(6)} %select_n.100, s32[512]{0:T(512)S(1)} %get-tuple-element.276, ...), kind=kOutput, calls=%fused_computation.28.clone.1 | convolution fusion | flops 206044672 | bytes 3692552 | tf_op jit(solution)/shard_map/while/body/eval_jaxpr/dot_general | solution.py:49
  63.5 1.0 fusion.36
  64.5 2.0 %fusion.37 = bf16[512,2048]{1,0:T(8,128)(2,1)} fusion(bf16[512,2048]{1,0:T(8,128)(2,1)} %get-tuple-element.255, s32[]{:T(128)S(6)} %select_n.100, f32[512,1536]{1,0:T(8,128)S(1)} %get-tuple-element.235, s32[1536]{0:T(1024)S(1)} %get-tuple-element.277, s32[1536]{0:T(1024)S(1)} %get-tuple-element.274, f32[512]{0:T(512)S(1)} %get-tuple-element.236, ...), kind=kOutput, calls=%fused_computation.10.clone.1 | convolution fusion | flops 206176256 | bytes 3694600 | tf_op jit(solution)/shard_map/while/body/eval_jaxpr/dot_general | solution.py:59
  66.6 1.8 %fusion.35 = (f32[512]{0:T(512)S(1)}, f32[512,1536]{1,0:T(8,128)S(1)}) fusion(bf16[1,1536,256]{2,1,0:T(8,128)(2,1)S(1)} %get-tuple-element.234, s32[]{:T(128)S(6)} %select_n.102, bf16[512,2048]{1,0:T(8,128)(2,1)} %get-tuple-element.272, s32[]{:T(128)S(6)} %select_n.100, s32[512]{0:T(512)S(1)} %get-tuple-element.276, ...), kind=kOutput, calls=%fused_computation.28.clone.1 | convolution fusion | flops 206044672 | bytes 3692552 | tf_op jit(solution)/shard_map/while/body/eval_jaxpr/dot_general | solution.py:49
  68.4 1.0 fusion.36
  69.4 2.0 %fusion.37 = bf16[512,2048]{1,0:T(8,128)(2,1)} fusion(bf16[512,2048]{1,0:T(8,128)(2,1)} %get-tuple-element.255, s32[]{:T(128)S(6)} %select_n.100, f32[512,1536]{1,0:T(8,128)S(1)} %get-tuple-element.235, s32[1536]{0:T(1024)S(1)} %get-tuple-element.277, s32[1536]{0:T(1024)S(1)} %get-tuple-element.274, f32[512]{0:T(512)S(1)} %get-tuple-element.236, ...), kind=kOutput, calls=%fused_computation.10.clone.1 | convolution fusion | flops 206176256 | bytes 3694600 | tf_op jit(solution)/shard_map/while/body/eval_jaxpr/dot_general | solution.py:59
  71.5 1.8 %fusion.35 = (f32[512]{0:T(512)S(1)}, f32[512,1536]{1,0:T(8,128)S(1)}) fusion(bf16[1,1536,256]{2,1,0:T(8,128)(2,1)S(1)} %get-tuple-element.234, s32[]{:T(128)S(6)} %select_n.102, bf16[512,2048]{1,0:T(8,128)(2,1)} %get-tuple-element.272, s32[]{:T(128)S(6)} %select_n.100, s32[512]{0:T(512)S(1)} %get-tuple-element.276, ...), kind=kOutput, calls=%fused_computation.28.clone.1 | convolution fusion | flops 206044672 | bytes 3692552 | tf_op jit(solution)/shard_map/while/body/eval_jaxpr/dot_general | solution.py:49
  73.3 1.0 fusion.36
  74.3 2.0 %fusion.37 = bf16[512,2048]{1,0:T(8,128)(2,1)} fusion(bf16[512,2048]{1,0:T(8,128)(2,1)} %get-tuple-element.255, s32[]{:T(128)S(6)} %select_n.100, f32[512,1536]{1,0:T(8,128)S(1)} %get-tuple-element.235, s32[1536]{0:T(1024)S(1)} %get-tuple-element.277, s32[1536]{0:T(1024)S(1)} %get-tuple-element.274, f32[512]{0:T(512)S(1)} %get-tuple-element.236, ...), kind=kOutput, calls=%fused_computation.10.clone.1 | convolution fusion | flops 206176256 | bytes 3694600 | tf_op jit(solution)/shard_map/while/body/eval_jaxpr/dot_general | solution.py:59
  76.4 1.8 %fusion.35 = (f32[512]{0:T(512)S(1)}, f32[512,1536]{1,0:T(8,128)S(1)}) fusion(bf16[1,1536,256]{2,1,0:T(8,128)(2,1)S(1)} %get-tuple-element.234, s32[]{:T(128)S(6)} %select_n.102, bf16[512,2048]{1,0:T(8,128)(2,1)} %get-tuple-element.272, s32[]{:T(128)S(6)} %select_n.100, s32[512]{0:T(512)S(1)} %get-tuple-element.276, ...), kind=kOutput, calls=%fused_computation.28.clone.1 | convolution fusion | flops 206044672 | bytes 3692552 | tf_op jit(solution)/shard_map/while/body/eval_jaxpr/dot_general | solution.py:49
  78.2 1.0 fusion.36
  79.2 2.0 %fusion.37 = bf16[512,2048]{1,0:T(8,128)(2,1)} fusion(bf16[512,2048]{1,0:T(8,128)(2,1)} %get-tuple-element.255, s32[]{:T(128)S(6)} %select_n.100, f32[512,1536]{1,0:T(8,128)S(1)} %get-tuple-element.235, s32[1536]{0:T(1024)S(1)} %get-tuple-element.277, s32[1536]{0:T(1024)S(1)} %get-tuple-element.274, f32[512]{0:T(512)S(1)} %get-tuple-element.236, ...), kind=kOutput, calls=%fused_computation.10.clone.1 | convolution fusion | flops 206176256 | bytes 3694600 | tf_op jit(solution)/shard_map/while/body/eval_jaxpr/dot_general | solution.py:59
  81.3 1.8 %fusion.35 = (f32[512]{0:T(512)S(1)}, f32[512,1536]{1,0:T(8,128)S(1)}) fusion(bf16[1,1536,256]{2,1,0:T(8,128)(2,1)S(1)} %get-tuple-element.234, s32[]{:T(128)S(6)} %select_n.102, bf16[512,2048]{1,0:T(8,128)(2,1)} %get-tuple-element.272, s32[]{:T(128)S(6)} %select_n.100, s32[512]{0:T(512)S(1)} %get-tuple-element.276, ...), kind=kOutput, calls=%fused_computation.28.clone.1 | convolution fusion | flops 206044672 | bytes 3692552 | tf_op jit(solution)/shard_map/while/body/eval_jaxpr/dot_general | solution.py:49
  84.1 2.0 %fusion.37 = bf16[512,2048]{1,0:T(8,128)(2,1)} fusion(bf16[512,2048]{1,0:T(8,128)(2,1)} %get-tuple-element.255, s32[]{:T(128)S(6)} %select_n.100, f32[512,1536]{1,0:T(8,128)S(1)} %get-tuple-element.235, s32[1536]{0:T(1024)S(1)} %get-tuple-element.277, s32[1536]{0:T(1024)S(1)} %get-tuple-element.274, f32[512]{0:T(512)S(1)} %get-tuple-element.236, ...), kind=kOutput, calls=%fused_computation.10.clone.1 | convolution fusion | flops 206176256 | bytes 3694600 | tf_op jit(solution)/shard_map/while/body/eval_jaxpr/dot_general | solution.py:59
  86.2 1.8 %fusion.35 = (f32[512]{0:T(512)S(1)}, f32[512,1536]{1,0:T(8,128)S(1)}) fusion(bf16[1,1536,256]{2,1,0:T(8,128)(2,1)S(1)} %get-tuple-element.234, s32[]{:T(128)S(6)} %select_n.102, bf16[512,2048]{1,0:T(8,128)(2,1)} %get-tuple-element.272, s32[]{:T(128)S(6)} %select_n.100, s32[512]{0:T(512)S(1)} %get-tuple-element.276, ...), kind=kOutput, calls=%fused_computation.28.clone.1 | convolution fusion | flops 206044672 | bytes 3692552 | tf_op jit(solution)/shard_map/while/body/eval_jaxpr/dot_general | solution.py:49
  89.0 2.0 %fusion.37 = bf16[512,2048]{1,0:T(8,128)(2,1)} fusion(bf16[512,2048]{1,0:T(8,128)(2,1)} %get-tuple-element.255, s32[]{:T(128)S(6)} %select_n.100, f32[512,1536]{1,0:T(8,128)S(1)} %get-tuple-element.235, s32[1536]{0:T(1024)S(1)} %get-tuple-element.277, s32[1536]{0:T(1024)S(1)} %get-tuple-element.274, f32[512]{0:T(512)S(1)} %get-tuple-element.236, ...), kind=kOutput, calls=%fused_computation.10.clone.1 | convolution fusion | flops 206176256 | bytes 3694600 | tf_op jit(solution)/shard_map/while/body/eval_jaxpr/dot_general | solution.py:59
  91.1 1.8 %fusion.35 = (f32[512]{0:T(512)S(1)}, f32[512,1536]{1,0:T(8,128)S(1)}) fusion(bf16[1,1536,256]{2,1,0:T(8,128)(2,1)S(1)} %get-tuple-element.234, s32[]{:T(128)S(6)} %select_n.102, bf16[512,2048]{1,0:T(8,128)(2,1)} %get-tuple-element.272, s32[]{:T(128)S(6)} %select_n.100, s32[512]{0:T(512)S(1)} %get-tuple-element.276, ...), kind=kOutput, calls=%fused_computation.28.clone.1 | convolution fusion | flops 206044672 | bytes 3692552 | tf_op jit(solution)/shard_map/while/body/eval_jaxpr/dot_general | solution.py:49
  92.9 1.0 fusion.36
  93.9 2.0 %fusion.37 = bf16[512,2048]{1,0:T(8,128)(2,1)} fusion(bf16[512,2048]{1,0:T(8,128)(2,1)} %get-tuple-element.255, s32[]{:T(128)S(6)} %select_n.100, f32[512,1536]{1,0:T(8,128)S(1)} %get-tuple-element.235, s32[1536]{0:T(1024)S(1)} %get-tuple-element.277, s32[1536]{0:T(1024)S(1)} %get-tuple-element.274, f32[512]{0:T(512)S(1)} %get-tuple-element.236, ...), kind=kOutput, calls=%fused_computation.10.clone.1 | convolution fusion | flops 206176256 | bytes 3694600 | tf_op jit(solution)/shard_map/while/body/eval_jaxpr/dot_general | solution.py:59
  96.0 1.8 %fusion.35 = (f32[512]{0:T(512)S(1)}, f32[512,1536]{1,0:T(8,128)S(1)}) fusion(bf16[1,1536,256]{2,1,0:T(8,128)(2,1)S(1)} %get-tuple-element.234, s32[]{:T(128)S(6)} %select_n.102, bf16[512,2048]{1,0:T(8,128)(2,1)} %get-tuple-element.272, s32[]{:T(128)S(6)} %select_n.100, s32[512]{0:T(512)S(1)} %get-tuple-element.276, ...), kind=kOutput, calls=%fused_computation.28.clone.1 | convolution fusion | flops 206044672 | bytes 3692552 | tf_op jit(solution)/shard_map/while/body/eval_jaxpr/dot_general | solution.py:49
  98.8 2.0 %fusion.37 = bf16[512,2048]{1,0:T(8,128)(2,1)} fusion(bf16[512,2048]{1,0:T(8,128)(2,1)} %get-tuple-element.255, s32[]{:T(128)S(6)} %select_n.100, f32[512,1536]{1,0:T(8,128)S(1)} %get-tuple-element.235, s32[1536]{0:T(1024)S(1)} %get-tuple-element.277, s32[1536]{0:T(1024)S(1)} %get-tuple-element.274, f32[512]{0:T(512)S(1)} %get-tuple-element.236, ...), kind=kOutput, calls=%fused_computation.10.clone.1 | convolution fusion | flops 206176256 | bytes 3694600 | tf_op jit(solution)/shard_map/while/body/eval_jaxpr/dot_general | solution.py:59
  100.9 1.8 %fusion.35 = (f32[512]{0:T(512)S(1)}, f32[512,1536]{1,0:T(8,128)S(1)}) fusion(bf16[1,1536,256]{2,1,0:T(8,128)(2,1)S(1)} %get-tuple-element.234, s32[]{:T(128)S(6)} %select_n.102, bf16[512,2048]{1,0:T(8,128)(2,1)} %get-tuple-element.272, s32[]{:T(128)S(6)} %select_n.100, s32[512]{0:T(512)S(1)} %get-tuple-element.276, ...), kind=kOutput, calls=%fused_computation.28.clone.1 | convolution fusion | flops 206044672 | bytes 3692552 | tf_op jit(solution)/shard_map/while/body/eval_jaxpr/dot_general | solution.py:49
  102.7 1.0 fusion.36
  103.7 2.0 %fusion.37 = bf16[512,2048]{1,0:T(8,128)(2,1)} fusion(bf16[512,2048]{1,0:T(8,128)(2,1)} %get-tuple-element.255, s32[]{:T(128)S(6)} %select_n.100, f32[512,1536]{1,0:T(8,128)S(1)} %get-tuple-element.235, s32[1536]{0:T(1024)S(1)} %get-tuple-element.277, s32[1536]{0:T(1024)S(1)} %get-tuple-element.274, f32[512]{0:T(512)S(1)} %get-tuple-element.236, ...), kind=kOutput, calls=%fused_computation.10.clone.1 | convolution fusion | flops 206176256 | bytes 3694600 | tf_op jit(solution)/shard_map/while/body/eval_jaxpr/dot_general | solution.py:59
  105.8 1.8 %fusion.35 = (f32[512]{0:T(512)S(1)}, f32[512,1536]{1,0:T(8,128)S(1)}) fusion(bf16[1,1536,256]{2,1,0:T(8,128)(2,1)S(1)} %get-tuple-element.234, s32[]{:T(128)S(6)} %select_n.102, bf16[512,2048]{1,0:T(8,128)(2,1)} %get-tuple-element.272, s32[]{:T(128)S(6)} %select_n.100, s32[512]{0:T(512)S(1)} %get-tuple-element.276, ...), kind=kOutput, calls=%fused_computation.28.clone.1 | convolution fusion | flops 206044672 | bytes 3692552 | tf_op jit(solution)/shard_map/while/body/eval_jaxpr/dot_general | solution.py:49
  108.6 2.0 %fusion.37 = bf16[512,2048]{1,0:T(8,128)(2,1)} fusion(bf16[512,2048]{1,0:T(8,128)(2,1)} %get-tuple-element.255, s32[]{:T(128)S(6)} %select_n.100, f32[512,1536]{1,0:T(8,128)S(1)} %get-tuple-element.235, s32[1536]{0:T(1024)S(1)} %get-tuple-element.277, s32[1536]{0:T(1024)S(1)} %get-tuple-element.274, f32[512]{0:T(512)S(1)} %get-tuple-element.236, ...), kind=kOutput, calls=%fused_computation.10.clone.1 | convolution fusion | flops 206176256 | bytes 3694600 | tf_op jit(solution)/shard_map/while/body/eval_jaxpr/dot_general | solution.py:59
  110.7 1.8 %fusion.35 = (f32[512]{0:T(512)S(1)}, f32[512,1536]{1,0:T(8,128)S(1)}) fusion(bf16[1,1536,256]{2,1,0:T(8,128)(2,1)S(1)} %get-tuple-element.234, s32[]{:T(128)S(6)} %select_n.102, bf16[512,2048]{1,0:T(8,128)(2,1)} %get-tuple-element.272, s32[]{:T(128)S(6)} %select_n.100, s32[512]{0:T(512)S(1)} %get-tuple-element.276, ...), kind=kOutput, calls=%fused_computation.28.clone.1 | convolution fusion | flops 206044672 | bytes 3692552 | tf_op jit(solution)/shard_map/while/body/eval_jaxpr/dot_general | solution.py:49
  113.5 2.0 %fusion.37 = bf16[512,2048]{1,0:T(8,128)(2,1)} fusion(bf16[512,2048]{1,0:T(8,128)(2,1)} %get-tuple-element.255, s32[]{:T(128)S(6)} %select_n.100, f32[512,1536]{1,0:T(8,128)S(1)} %get-tuple-element.235, s32[1536]{0:T(1024)S(1)} %get-tuple-element.277, s32[1536]{0:T(1024)S(1)} %get-tuple-element.274, f32[512]{0:T(512)S(1)} %get-tuple-element.236, ...), kind=kOutput, calls=%fused_computation.10.clone.1 | convolution fusion | flops 206176256 | bytes 3694600 | tf_op jit(solution)/shard_map/while/body/eval_jaxpr/dot_general | solution.py:59
  115.6 1.8 %fusion.35 = (f32[512]{0:T(512)S(1)}, f32[512,1536]{1,0:T(8,128)S(1)}) fusion(bf16[1,1536,256]{2,1,0:T(8,128)(2,1)S(1)} %get-tuple-element.234, s32[]{:T(128)S(6)} %select_n.102, bf16[512,2048]{1,0:T(8,128)(2,1)} %get-tuple-element.272, s32[]{:T(128)S(6)} %select_n.100, s32[512]{0:T(512)S(1)} %get-tuple-element.276, ...), kind=kOutput, calls=%fused_computation.28.clone.1 | convolution fusion | flops 206044672 | bytes 3692552 | tf_op jit(solution)/shard_map/while/body/eval_jaxpr/dot_general | solution.py:49
  118.4 2.0 %fusion.37 = bf16[512,2048]{1,0:T(8,128)(2,1)} fusion(bf16[512,2048]{1,0:T(8,128)(2,1)} %get-tuple-element.255, s32[]{:T(128)S(6)} %select_n.100, f32[512,1536]{1,0:T(8,128)S(1)} %get-tuple-element.235, s32[1536]{0:T(1024)S(1)} %get-tuple-element.277, s32[1536]{0:T(1024)S(1)} %get-tuple-element.274, f32[512]{0:T(512)S(1)} %get-tuple-element.236, ...), kind=kOutput, calls=%fused_computation.10.clone.1 | convolution fusion | flops 206176256 | bytes 3694600 | tf_op jit(solution)/shard_map/while/body/eval_jaxpr/dot_general | solution.py:59
  120.5 1.8 %fusion.35 = (f32[512]{0:T(512)S(1)}, f32[512,1536]{1,0:T(8,128)S(1)}) fusion(bf16[1,1536,256]{2,1,0:T(8,128)(2,1)S(1)} %get-tuple-element.234, s32[]{:T(128)S(6)} %select_n.102, bf16[512,2048]{1,0:T(8,128)(2,1)} %get-tuple-element.272, s32[]{:T(128)S(6)} %select_n.100, s32[512]{0:T(512)S(1)} %get-tuple-element.276, ...), kind=kOutput, calls=%fused_computation.28.clone.1 | convolution fusion | flops 206044672 | bytes 3692552 | tf_op jit(solution)/shard_map/while/body/eval_jaxpr/dot_general | solution.py:49
  122.3 1.0 fusion.36
  123.3 2.0 %fusion.37 = bf16[512,2048]{1,0:T(8,128)(2,1)} fusion(bf16[512,2048]{1,0:T(8,128)(2,1)} %get-tuple-element.255, s32[]{:T(128)S(6)} %select_n.100, f32[512,1536]{1,0:T(8,128)S(1)} %get-tuple-element.235, s32[1536]{0:T(1024)S(1)} %get-tuple-element.277, s32[1536]{0:T(1024)S(1)} %get-tuple-element.274, f32[512]{0:T(512)S(1)} %get-tuple-element.236, ...), kind=kOutput, calls=%fused_computation.10.clone.1 | convolution fusion | flops 206176256 | bytes 3694600 | tf_op jit(solution)/shard_map/while/body/eval_jaxpr/dot_general | solution.py:59
  125.4 1.8 %fusion.35 = (f32[512]{0:T(512)S(1)}, f32[512,1536]{1,0:T(8,128)S(1)}) fusion(bf16[1,1536,256]{2,1,0:T(8,128)(2,1)S(1)} %get-tuple-element.234, s32[]{:T(128)S(6)} %select_n.102, bf16[512,2048]{1,0:T(8,128)(2,1)} %get-tuple-element.272, s32[]{:T(128)S(6)} %select_n.100, s32[512]{0:T(512)S(1)} %get-tuple-element.276, ...), kind=kOutput, calls=%fused_computation.28.clone.1 | convolution fusion | flops 206044672 | bytes 3692552 | tf_op jit(solution)/shard_map/while/body/eval_jaxpr/dot_general | solution.py:49
  128.2 2.0 %fusion.37 = bf16[512,2048]{1,0:T(8,128)(2,1)} fusion(bf16[512,2048]{1,0:T(8,128)(2,1)} %get-tuple-element.255, s32[]{:T(128)S(6)} %select_n.100, f32[512,1536]{1,0:T(8,128)S(1)} %get-tuple-element.235, s32[1536]{0:T(1024)S(1)} %get-tuple-element.277, s32[1536]{0:T(1024)S(1)} %get-tuple-element.274, f32[512]{0:T(512)S(1)} %get-tuple-element.236, ...), kind=kOutput, calls=%fused_computation.10.clone.1 | convolution fusion | flops 206176256 | bytes 3694600 | tf_op jit(solution)/shard_map/while/body/eval_jaxpr/dot_general | solution.py:59
  130.3 1.8 %fusion.35 = (f32[512]{0:T(512)S(1)}, f32[512,1536]{1,0:T(8,128)S(1)}) fusion(bf16[1,1536,256]{2,1,0:T(8,128)(2,1)S(1)} %get-tuple-element.234, s32[]{:T(128)S(6)} %select_n.102, bf16[512,2048]{1,0:T(8,128)(2,1)} %get-tuple-element.272, s32[]{:T(128)S(6)} %select_n.100, s32[512]{0:T(512)S(1)} %get-tuple-element.276, ...), kind=kOutput, calls=%fused_computation.28.clone.1 | convolution fusion | flops 206044672 | bytes 3692552 | tf_op jit(solution)/shard_map/while/body/eval_jaxpr/dot_general | solution.py:49
  133.1 2.0 %fusion.37 = bf16[512,2048]{1,0:T(8,128)(2,1)} fusion(bf16[512,2048]{1,0:T(8,128)(2,1)} %get-tuple-element.255, s32[]{:T(128)S(6)} %select_n.100, f32[512,1536]{1,0:T(8,128)S(1)} %get-tuple-element.235, s32[1536]{0:T(1024)S(1)} %get-tuple-element.277, s32[1536]{0:T(1024)S(1)} %get-tuple-element.274, f32[512]{0:T(512)S(1)} %get-tuple-element.236, ...), kind=kOutput, calls=%fused_computation.10.clone.1 | convolution fusion | flops 206176256 | bytes 3694600 | tf_op jit(solution)/shard_map/while/body/eval_jaxpr/dot_general | solution.py:59
  (38 shorter events, 11.0 us)
Async XLA Ops:
  0.0 17.0 %copy-start = (s32[64]{0:T(128)S(1)}, s32[64]{0:T(128)}, u32[]{:S(2)}) copy-start(s32[64]{0:T(128)} %param.9) | copy-start | bytes 772
  13.2 21.5 %collective-permute-start = (bf16[2,512,256]{2,1,0:T(8,128)(2,1)S(1)}, bf16[2,512,256]{2,1,0:T(8,128)(2,1)S(1)}, u32[]{:S(2)}, u32[]{:S(2)}) collective-permute-start(bf16[2,512,256]{2,1,0:T(8,128)(2,1)S(1)} %bitcast.20), channel_id=1, source_target_pairs={{0,4},{4,8},{8,12},{12,16},{16,20},{20,24},{24,28},{28,32},{32,36}... | collective-permute-start | bytes 1572872 | tf_op jit(solution)/shard_map/ppermute | solution.py:13
  34.7 20.3 %collective-permute-start.1 = (bf16[2,512,256]{2,1,0:T(8,128)(2,1)S(1)}, bf16[2,512,256]{2,1,0:T(8,128)(2,1)S(1)}, u32[]{:S(2)}, u32[]{:S(2)}) collective-permute-start(bf16[2,512,256]{2,1,0:T(8,128)(2,1)S(1)} %collective-permute-done), channel_id=1, source_target_pairs={{0,4},{4,8},{8,12},{12,16},{16,20},{20,24},{24,28},{28,32},{32,36}... | collective-permute-start | bytes 1572872 | tf_op jit(solution)/shard_map/ppermute | solution.py:13
where the time goes:
time: 136 us; the launch traced here: 135 us
  matrix products  60.9 us (45%)
  waiting for transfers between devices  35.5 us (26%)
  other arithmetic  17.4 us (13%)
  blocking collectives  11.2 us (8%)
  starting transfers between devices  5.73 us (4%)
  local copies, waits for them, and re-layouts  4.13 us (3%)
    ppermute x2, waiting for transfers between devices, passed_along(): lax.ppermute(value, axis, [(source, source + steps) for source in range(l...  35.5 us
    dot_general x16, matrix products, one_head(): jnp.dot(rounded, value_head, preferred_element_type=jnp.float32) / total  32.2 us
    dot_general x16, matrix products, one_head(): lax.dot_general(query_head, key_head, (((1,), (1,)), ((), ())), preferred...  28.8 us
    reduce_sum x16, other arithmetic, one_head(): total = jnp.sum(weights, axis=1, keepdims=True)  15.8 us
    all_to_all x1, blocking collectives, per_device(): lax.all_to_all(stacked, 'head', split_axis=2, concat_axis=1, tiled=True)  11.2 us
    ppermute x2, starting transfers between devices, passed_along(): lax.ppermute(value, axis, [(source, source + steps) for source in range(l...  5.73 us
  transfers between devices with their start and end apart: 2, of which 2 were waited for; matrix products, arithmetic and copies ran while one was open for 0% of the time, Pallas kernels for 0%

commit v1 on v0

v1 whole, which is shorter than its diff:
```python
import functools

import jax
import jax.numpy as jnp
from jax import lax
from jax.experimental import pallas as pl
from jax.experimental.pallas import tpu as pltpu
from jax.sharding import PartitionSpec as P

HD = 128
SCALE = 128**-0.5 * 1.4426950408889634
NEG = -1e30
BF16 = jnp.bfloat16
F32 = jnp.float32
MESH = pl.DeviceIdType.MESH
UNROLL = 4


def dot(a, b, ca, cb):
    return lax.dot_general(a, b, (((ca,), (cb,)), ((), ())), preferred_element_type=F32)


def kernel(
    n, q_hbm, k_hbm, v_hbm, len_hbm, out, qv, ko, vo, k1a, v1a, k1b, v1b, k2h, v2h, k2l, v2l, krel, vrel,
    bo, b1a, b1b, b2h, b2l, acc, top, sb, lens, loc, a_send, a_recv, s1, r1, s2, r2, sr, rr, sf,
):
    c = lax.axis_index("ctx")
    h = lax.axis_index("head")
    hx = [h, (h // 2) * 2 + 1 - h % 2, (1 - h // 2) * 2 + h % 2, 3 - h]
    hh = h // 2
    z = c % 8
    inner = c < n - 8
    has_next = c < n - 1
    has_prev = c > 0
    to_relay = (z == 6) & inner
    relays = (z == 3) & inner
    passes = has_prev & has_next & (z != 7)

    def cols(g):
        return pl.ds(pl.multiple_of(g * 256, 256), 256)

    def rows(b):
        return pl.ds(pl.multiple_of(b * 128, 128), 128)

    src, own, rel = (k_hbm, v_hbm), (ko, vo), (krel, vrel)
    one = ((k1a, v1a), (k1a, v1a), (k1b, v1b), (k1b, v1b))
    two = (((k2l, v2l), (k2h, v2h)), ((k2h, v2h), (k2l, v2l)))

    def remote(a, b, send, recv, device):
        return pltpu.make_async_remote_copy(
            a, b, send, recv, device_id=device, device_id_type=MESH
        )

    def exchange(d):
        return [
            remote(src[t].at[:, cols(hx[d])], own[t].at[rows(h)], a_send.at[d, t], a_recv.at[d, t], (c, hx[d]))
            for t in (0, 1)
        ]

    def piece(d, t):
        return src[t].at[:, cols(h)] if d == 0 else own[t].at[rows(hx[d])]

    def first(d):
        return [
            remote(piece(d, t), one[d][t].at[rows(hx[d] % 2)], s1.at[d, t], r1.at[d, t], (c + 1, h))
            for t in (0, 1)
        ]

    def second(d, half):
        return [
            remote(
                one[d][t].at[rows(hx[d] % 2)], two[half][d // 2][t].at[rows(hx[d] % 2)],
                s2.at[d, t], r2.at[d, t], (c + 1, h),
            )
            for t in (0, 1)
        ]

    def back(d):
        return [
            remote(piece(d, t), rel[t].at[d], sr.at[d, t], rr.at[d, t], (c - 3, h))
            for t in (0, 1)
        ]

    def onward(d, half):
        return [
            remote(
                rel[t].at[d], two[half][d // 2][t].at[rows(hx[d] % 2)],
                sf.at[d, t], r2.at[d, t], (c + 5, h),
            )
            for t in (0, 1)
        ]

    def start(copies):
        for copy in copies:
            copy.start()

    def taken(copies):
        for copy in copies:
            copy.wait_recv()

    barrier = pltpu.get_barrier_semaphore()

    def greet(device):
        pl.semaphore_signal(barrier, 1, device_id=device, device_id_type=MESH)

    for d in (1, 2, 3):
        greet((c, hx[d]))

    @pl.when(has_prev)
    def _():
        greet((c - 1, h))

    @pl.when(relays)
    def _():
        greet((c + 3, h))

    @pl.when((z == 0) & has_prev)
    def _():
        greet((c - 5, h))

    local = [
        pltpu.make_async_copy(len_hbm, lens, loc.at[0]),
        pltpu.make_async_copy(k_hbm.at[:, cols(h)], ko.at[rows(h)], loc.at[1]),
        pltpu.make_async_copy(v_hbm.at[:, cols(h)], vo.at[rows(h)], loc.at[2]),
        pltpu.make_async_copy(q_hbm, qv, loc.at[3]),
    ]
    start(local)
    others = jnp.where(has_next, 1, 0) + jnp.where(to_relay, 1, 0) + jnp.where(relays, 1, 0)
    pl.semaphore_wait(barrier, 3 + others)

    @pl.when(has_next)
    def _():
        start(first(0))

    @pl.when(to_relay)
    def _():
        start(back(0))

    for d in (1, 2, 3):
        start(exchange(d))

    @pl.when(c == 0)
    def _():
        for ref in (k1a, v1a, k1b, v1b):
            ref[...] = jnp.zeros((256, 256), BF16)

    @pl.when(c <= 1)
    def _():
        for ref in (k2h, v2h, k2l, v2l):
            ref[...] = jnp.zeros((256, 256), BF16)

    local[0].wait()
    tok = c * 512

    def later(i, carry):
        end, begin = carry
        for u in range(8):
            end = end + lens[i * 8 + u]
            begin = jnp.where(lanes >= end, end, begin)
        return end, begin

    lanes = tok + lax.broadcasted_iota(jnp.int32, (8, 512), 1)
    _, begin = lax.fori_loop(0, 8, later, (jnp.int32(0), jnp.zeros((8, 512), jnp.int32)))
    begin = begin.astype(F32)

    def masks():
        spread = lax.broadcasted_iota(jnp.int32, (128, 128), 1)
        for r in range(0, 512, 128):
            lead = jnp.tile(begin[:, r : r + 128], (16, 1)).T.astype(jnp.int32)
            pos = tok + r + lax.broadcasted_iota(jnp.int32, (128, 128), 0)
            for ref, base, size in (
                (bo, tok, 512), (b1a, tok - 512 + 256 * hh, 256), (b1b, tok - 256 - 256 * hh, 256),
                (b2h, tok - 768, 256), (b2l, tok - 1024, 256),
            ):
                if ref is b2l and r >= 256:
                    continue
                for k in range(0, size, 128):
                    key = base + k + spread
                    allowed = lead <= key
                    if ref is bo:
                        allowed = allowed & (key <= pos)
                    ref[r : r + 128, k : k + 128] = jnp.where(allowed, 0.0, NEG)

    for d in (1, 2, 3):
        taken(exchange(d))

        @pl.when(has_next)
        def _():
            start(first(d))

        @pl.when(to_relay)
        def _():
            start(back(d))

        if d == 1:
            masks()

    for copy in local[1:]:
        copy.wait()

    ones = {size: jnp.ones((size, HD), BF16) for size in (256, 512)}

    def stage(kw, vw, bias, tiles, opening=False, between=None):
        def scores(head, slot):
            shared = pl.ds(pl.multiple_of(head // 8 * HD, HD), HD)
            for r, nr, nk, _ in tiles:
                q = qv[r : r + nr, pl.ds(pl.multiple_of(head * HD, HD), HD)]
                sb[slot, r : r + nr, 0:nk] = dot(q, kw[0:nk, shared], 1, 1)

        def mix(head, slot):
            shared = pl.ds(pl.multiple_of(head // 8 * HD, HD), HD)
            for r, nr, nk, closing in tiles:
                s = sb[slot, r : r + nr, 0:nk] * SCALE + bias[r : r + nr, 0:nk]
                high = jnp.max(s, axis=1, keepdims=True)
                if opening:
                    new = jnp.broadcast_to(high, (nr, HD))
                else:
                    old = top[head, r : r + nr, :]
                    new = jnp.maximum(old, high)
                p = jnp.exp2(s - jnp.tile(new, (1, nk // HD))).astype(BF16)
                v = jnp.concatenate([vw[0:nk, shared], ones[nk]], axis=1)
                o = dot(p, v, 1, 0)
                if not opening:
                    o = acc[head, r : r + nr, :] * jnp.tile(jnp.exp2(old - new), (1, 2)) + o
                if closing:
                    out[r : r + nr, pl.ds(pl.multiple_of(head * HD, HD), HD)] = (
                        o[:, 0:HD] / o[:, HD : 2 * HD]
                    ).astype(BF16)
                else:
                    acc[head, r : r + nr, :] = o
                    top[head, r : r + nr, :] = new

        scores(0, 0)

        def step(i, carry):
            for u in range(UNROLL):
                head = i * UNROLL + u
                scores(lax.rem(head + 1, 16), (u + 1) % 2)
                mix(head, u % 2)
            if between is not None:

                @pl.when(i == 0)
                def _():
                    between()

            return carry

        lax.fori_loop(0, 16 // UNROLL, step, 0)

    def relay(d):
        @pl.when(relays)
        def _():
            taken(back(d))

        for half in (0, 1):

            @pl.when(relays & (hh == half))
            def _():
                start(onward(d, half))

    def forward(cond, half, pieces):
        @pl.when(cond & has_prev & (hh == half))
        def _():
            for d in pieces:
                if d > 1:
                    taken(first(d))

        @pl.when(cond & passes & (hh == half))
        def _():
            for d in pieces:
                start(second(d, half))

    def forward_early(cond):
        forward(cond, 0, (2,))
        forward(cond, 1, (0, 1))

    def forward_late(cond):
        forward(cond, 0, (3, 1, 0))
        forward(cond, 1, (2, 3))

    stage(ko, vo, bo, [(0, 256, 256, False), (256, 256, 512, False)], True, lambda: relay(0))
    relay(1)

    @pl.when(has_prev)
    def _():
        taken(first(0))
        taken(first(1))

    forward_early(z != 0)

    def middle():
        relay(2)
        forward_late(z != 0)
        forward_early(z == 0)

    stage(k1a, v1a, b1a, [(0, 512, 256, False)], between=middle)
    relay(3)
    forward_late(z == 0)
    stage(k1b, v1b, b1b, [(0, 512, 256, False)])

    def landed(half, pieces):
        @pl.when((c > 1) & (hh == half))
        def _():
            for d in pieces:
                taken(second(d, half))

    landed(0, (2, 3))
    landed(1, (0, 1))
    stage(k2h, v2h, b2h, [(0, 256, 256, False), (256, 256, 256, True)])
    landed(0, (0, 1))
    landed(1, (2, 3))
    stage(k2l, v2l, b2l, [(0, 256, 256, True)])

    for d in (1, 2, 3):
        for copy in exchange(d):
            copy.wait_send()
    for d in range(4):

        @pl.when(has_next)
        def _():
            for copy in first(d):
                copy.wait_send()

        @pl.when(passes)
        def _():
            for copy in second(d, 0):
                copy.wait_send()

        @pl.when(to_relay)
        def _():
            for copy in back(d):
                copy.wait_send()

        @pl.when(relays)
        def _():
            for copy in onward(d, 0):
                copy.wait_send()


def per_device(n, queries, keys, values, lengths):
    hbm = pl.BlockSpec(memory_space=pltpu.HBM)
    sems = pltpu.SemaphoreType.DMA((4, 2))
    return pl.pallas_call(
        functools.partial(kernel, n),
        out_shape=jax.ShapeDtypeStruct(queries.shape, BF16),
        in_specs=[hbm] * 4,
        out_specs=pl.BlockSpec(memory_space=pltpu.VMEM),
        scratch_shapes=[pltpu.VMEM((512, 2048), BF16)]
        + [pltpu.VMEM((512, 256), BF16)] * 2
        + [pltpu.VMEM((256, 256), BF16)] * 8
        + [pltpu.VMEM((4, 128, 256), BF16)] * 2
        + [pltpu.VMEM((512, 512), F32)]
        + [pltpu.VMEM((512, 256), F32)] * 3
        + [pltpu.VMEM((256, 256), F32)]
        + [
            pltpu.VMEM((16, 512, 256), F32),
            pltpu.VMEM((16, 512, 128), F32),
            pltpu.VMEM((2, 512, 512), F32),
            pltpu.SMEM((64,), jnp.int32),
            pltpu.SemaphoreType.DMA((4,)),
        ]
        + [sems] * 9,
        compiler_params=pltpu.CompilerParams(
            collective_id=0, has_side_effects=True, vmem_limit_bytes=58 * 2**20
        ),
    )(queries, keys, values, lengths)


def solution(mesh):
    placed = (P("ctx", "head"), P(("ctx", "head"), None), P(("ctx", "head"), None), P())
    return jax.shard_map(
        functools.partial(per_device, mesh.shape["ctx"]),
        mesh=mesh,
        in_specs=placed,
        out_specs=P("ctx", "head"),
        check_vma=False,
    )
```

time: 136 us -> 45.3 us (0.33)
  matrix products: 60.9 us -> 0 us
  Pallas kernels: 0 us -> 41.5 us
  waiting for transfers between devices: 35.5 us -> 0 us
  other arithmetic: 17.4 us -> 0 us
  blocking collectives: 11.2 us -> 0 us
  starting transfers between devices: 5.73 us -> 0 us
    dot_general x32 -> x0, matrix products: 60.9 us -> none  [the longest x16 32.2 us: one_head(): jnp.dot(rounded, value_head, preferred_element_type=jnp.float32) / total]
    pallas_call x0 -> x1, Pallas kernels: none -> 41.5 us  [per_device(): pl.pallas_call(functools.partial(kernel, n), out_shape=jax.ShapeDtypeStru...]
    ppermute x2 -> x0, waiting for transfers between devices: 35.5 us -> none  [passed_along(): lax.ppermute(value, axis, [(source, source + steps) for source in range(l...]
    reduce_sum x18 -> x0, other arithmetic: 16 us -> none  [the longest x16 15.8 us: one_head(): total = jnp.sum(weights, axis=1, keepdims=True)]
    all_to_all x1 -> x0, blocking collectives: 11.2 us -> none  [per_device(): lax.all_to_all(stacked, 'head', split_axis=2, concat_axis=1, tiled=True)]
    ppermute x2 -> x0, starting transfers between devices: 5.73 us -> none  [passed_along(): lax.ppermute(value, axis, [(source, source + steps) for source in range(l...]
    unnamed x2 -> x1, local copies, waits for them, and re-layouts: 0.01 us -> 3.16 us
    slice x16 -> x0, local copies, waits for them, and re-layouts: 1.63 us -> none  [one_head(): value_head = lax.dynamic_slice_in_dim(window[1], shared, HD, 1)]
  transfers between devices with their start and end apart: 2 -> 0, of which waited for: 2 -> 0; matrix products, arithmetic and copies ran while one was open for 0% -> 0% of each run, Pallas kernels for 0% -> 0%
where the time goes in v1:
time: 45.3 us; the launch traced here: 44.7 us
  Pallas kernels  41.5 us (92%)
  local copies, waits for them, and re-layouts  3.16 us (7%)
    pallas_call x1, Pallas kernels, per_device(): pl.pallas_call(functools.partial(kernel, n), out_shape=jax.ShapeDtypeStru...  41.5 us
    unnamed x1, local copies, waits for them, and re-layouts  3.16 us

profile of v1, /device:TPU:16, one launch (start us, length us, event | category | flops | bytes accessed | tf_op | source)
XLA Modules:
  0.0 44.7 jit_solution(9203645206040544992)
XLA Ops:
  0.0 41.5 %shard_map.46 = bf16[512,2048]{1,0:T(8,128)(2,1)} custom-call(bf16[512,2048]{1,0:T(8,128)(2,1)} %q_hbm.1, bf16[128,1024]{1,0:T(8,128)(2,1)} %k_hbm.1, bf16[128,1024]{1,0:T(8,128)(2,1)} %v_hbm.1, s32[64]{0:T(128)} %len_hbm.1), custom_call_target="tpu_custom_call" | custom-call | tf_op jit(solution)/shard_map/pallas_call | solution.py:343
  41.5 3.2 %copy.6 = bf16[512,2048]{1,0:T(8,128)(2,1)} copy(bf16[512,2048]{1,0:T(8,128)(2,1)} %shard_map.46) | data formatting | bytes 4194304

commit v2 on v1

v2 whole, which is shorter than its diff:
```python
import functools

import jax
import jax.numpy as jnp
from jax import lax
from jax.experimental import pallas as pl
from jax.experimental.pallas import tpu as pltpu
from jax.sharding import PartitionSpec as P

HD = 128
SCALE = 128**-0.5 * 1.4426950408889634
NEG = -1e30
BF16 = jnp.bfloat16
F32 = jnp.float32
MESH = pl.DeviceIdType.MESH
PARTS = 4


def dot(a, b, ca, cb):
    return lax.dot_general(a, b, (((ca,), (cb,)), ((), ())), preferred_element_type=F32)


def kernel(
    n, q_hbm, k_hbm, v_hbm, len_hbm, out, qv, ko, vo, k1a, v1a, k1b, v1b, k2h, v2h, k21, v21, k20, v20,
    bo, b1a, b1b, b2h, b21, b20, acc, top, sb, lens, loc, a_send, a_recv, s1, r1, s2, r2, flush, ov2, ov1, ov0,
):
    c = lax.axis_index("ctx")
    h = lax.axis_index("head")
    hx = [h, (h // 2) * 2 + 1 - h % 2, (1 - h // 2) * 2 + h % 2, 3 - h]
    hh = h // 2
    z = c % 8
    has_next = c < n - 1
    has_prev = c > 0
    passes = has_prev & has_next

    def cols(g):
        return pl.ds(pl.multiple_of(g * 256, 256), 256)

    def rows(b):
        return pl.ds(pl.multiple_of(b * 128, 128), 128)

    src, own = (k_hbm, v_hbm), (ko, vo)
    one = ((k1a, v1a), (k1a, v1a), (k1b, v1b), (k1b, v1b))
    low = ((k20, v20), (k21, v21))

    def remote(a, b, send, recv, device):
        return pltpu.make_async_remote_copy(
            a, b, send, recv, device_id=device, device_id_type=MESH
        )

    def exchange(d):
        return [
            remote(src[t].at[:, cols(hx[d])], own[t].at[rows(h)], a_send.at[d, t], a_recv.at[d, t], (c, hx[d]))
            for t in (0, 1)
        ]

    def piece(d, t):
        return src[t].at[:, cols(h)] if d == 0 else own[t].at[rows(hx[d])]

    def first(d):
        return [
            remote(piece(d, t), one[d][t].at[rows(hx[d] % 2)], s1.at[d, t], r1.at[d, t], (c + 1, h))
            for t in (0, 1)
        ]

    def second(d, b=None):
        return [
            remote(
                one[d][t].at[rows(hx[d] % 2)], (k2h, v2h)[t].at[rows(hx[d] % 2)] if b is None else low[b][t],
                s2.at[d, t], r2.at[d, t], (c + 1, h),
            )
            for t in (0, 1)
        ]

    def start(copies):
        for copy in copies:
            copy.start()

    def taken(copies):
        for copy in copies:
            copy.wait_recv()

    barrier = pltpu.get_barrier_semaphore()

    def greet(device):
        pl.semaphore_signal(barrier, 1, device_id=device, device_id_type=MESH)

    for d in (1, 2, 3):
        greet((c, hx[d]))

    @pl.when(has_prev)
    def _():
        greet((c - 1, h))

    local = [
        pltpu.make_async_copy(len_hbm, lens, loc.at[0]),
        pltpu.make_async_copy(k_hbm.at[:, cols(h)], ko.at[rows(h)], loc.at[1]),
        pltpu.make_async_copy(v_hbm.at[:, cols(h)], vo.at[rows(h)], loc.at[2]),
        pltpu.make_async_copy(q_hbm, qv, loc.at[3]),
    ]
    start(local)
    pl.semaphore_wait(barrier, 3 + jnp.where(has_next, 1, 0))

    @pl.when(has_next)
    def _():
        start(first(0))

    for d in (1, 2, 3):
        start(exchange(d))

    @pl.when(c == 0)
    def _():
        for ref in (k1a, v1a, k1b, v1b):
            ref[...] = jnp.zeros((256, 256), BF16)

    @pl.when(c <= 1)
    def _():
        for ref in (k2h, v2h, k21, v21, k20, v20):
            ref[...] = jnp.zeros(ref.shape, BF16)

    local[0].wait()
    tok = c * 512

    def later(i, carry):
        end, begin = carry
        for u in range(8):
            end = end + lens[i * 8 + u]
            begin = jnp.where(lanes >= end, end, begin)
        return end, begin

    lanes = tok + lax.broadcasted_iota(jnp.int32, (8, 512), 1)
    _, begin = lax.fori_loop(0, 8, later, (jnp.int32(0), jnp.zeros((8, 512), jnp.int32)))
    begin = begin.astype(F32)

    def masks():
        spread = lax.broadcasted_iota(jnp.int32, (128, 128), 1)
        for r in range(0, 512, 128):
            lead = jnp.tile(begin[:, r : r + 128], (16, 1)).T.astype(jnp.int32)
            pos = tok + r + lax.broadcasted_iota(jnp.int32, (128, 128), 0)
            for ref, base, size in (
                (bo, tok, 512), (b1a, tok - 512 + 256 * hh, 256), (b1b, tok - 256 - 256 * hh, 256),
                (b2h, tok - 768, 256), (b21, tok - 896, 128), (b20, tok - 1024, 128),
            ):
                if (ref is b21 and r >= 256) or (ref is b20 and r >= 128):
                    continue
                for k in range(0, size, 128):
                    key = base + k + spread
                    allowed = lead <= key
                    if ref is bo:
                        allowed = allowed & (key <= pos)
                    ref[r : r + 128, k : k + 128] = jnp.where(allowed, 0.0, NEG)

    for d in (1, 2, 3):
        taken(exchange(d))

        @pl.when(has_next)
        def _():
            start(first(d))

        if d == 1:
            masks()

    for copy in local[1:]:
        copy.wait()

    ones = {size: jnp.ones((size, HD), BF16) for size in (128, 256, 512)}

    def stage(kw, vw, bias, tiles, opening=False, between=None, unroll=8):
        def scores(head, slot):
            shared = pl.ds(pl.multiple_of(head // 8 * HD, HD), HD)
            for r, nr, k, nk, _ in tiles:
                q = qv[r : r + nr, pl.ds(pl.multiple_of(head * HD, HD), HD)]
                sb[slot, r : r + nr, 0:nk] = dot(q, kw[k : k + nk, shared], 1, 1)

        def mix(head, slot):
            shared = pl.ds(pl.multiple_of(head // 8 * HD, HD), HD)
            for r, nr, k, nk, closing in tiles:
                s = sb[slot, r : r + nr, 0:nk] * SCALE + bias[r : r + nr, k : k + nk]
                high = jnp.max(s, axis=1, keepdims=True)
                if opening:
                    new = jnp.broadcast_to(high, (nr, HD))
                else:
                    old = top[head, r : r + nr, :]
                    new = jnp.maximum(old, high)
                p = jnp.exp2(s - jnp.tile(new, (1, nk // HD))).astype(BF16)
                v = jnp.concatenate([vw[k : k + nk, shared], ones[nk]], axis=1)
                o = dot(p, v, 1, 0)
                if not opening:
                    o = acc[head, r : r + nr, :] * jnp.tile(jnp.exp2(old - new), (1, 2)) + o
                if closing is not None:
                    closing[:, pl.ds(pl.multiple_of(head * HD, HD), HD)] = (
                        o[:, 0:HD] / o[:, HD : 2 * HD]
                    ).astype(BF16)
                else:
                    acc[head, r : r + nr, :] = o
                    top[head, r : r + nr, :] = new

        scores(0, 0)

        def step(i, carry):
            for u in range(unroll):
                head = i * unroll + u
                scores(lax.rem(head + 1, 16), (u + 1) % 2)
                mix(head, u % 2)
            if between is not None:

                @pl.when(i == 0)
                def _():
                    between()

            return carry

        lax.fori_loop(0, 16 // unroll, step, 0)

    def forward(cond, half, pieces):
        @pl.when(cond & has_prev & (hh == half))
        def _():
            for d in pieces:
                if d > 1:
                    taken(first(d))

        @pl.when(cond & passes & (hh == half))
        def _():
            for d in pieces:
                if d // 2 != half:
                    start(second(d))

        for b in (1, 0):
            for d in pieces:
                if d // 2 == half:

                    @pl.when(cond & passes & (hh == half) & (hx[d] == b))
                    def _():
                        start(second(d, b))

    def forward_early(cond):
        forward(cond, 0, (2,))
        forward(cond, 1, (0, 1))

    def forward_late(cond):
        forward(cond, 0, (3, 1, 0))
        forward(cond, 1, (2, 3))

    stage(ko, vo, bo, [(0, 256, 0, 256, None), (256, 256, 0, 512, None)], True)

    @pl.when(has_prev)
    def _():
        taken(first(0))
        taken(first(1))

    forward_early(z != 0)

    def middle():
        forward_late(z != 0)
        forward_early(z == 0)

    stage(k1a, v1a, b1a, [(0, 512, 0, 256, None)], between=middle)
    forward_late(z == 0)
    stage(k1b, v1b, b1b, [(0, 512, 0, 256, None)])

    def landed(half, pieces):
        @pl.when((c > 1) & (hh == half))
        def _():
            for d in pieces:
                taken(second(d))

    def landed_low(b):
        for half in (0, 1):
            for d in (2 * half, 2 * half + 1):

                @pl.when((c > 1) & (hh == half) & (hx[d] == b))
                def _():
                    taken(second(d, b))

    def flushed(i, ref, r):
        return pltpu.make_async_copy(ref, out.at[r : r + ref.shape[0]], flush.at[i])

    landed(0, (2, 3))
    landed(1, (0, 1))
    stage(k2h, v2h, b2h, [(0, 256, 0, 256, None), (256, 256, 0, 256, ov2)])
    flushed(0, ov2, 256).start()
    landed_low(1)
    stage(k21, v21, b21, [(0, 128, 0, 128, None), (128, 128, 0, 128, ov1)], unroll=16)
    flushed(1, ov1, 128).start()
    landed_low(0)
    stage(k20, v20, b20, [(0, 128, 0, 128, ov0)], unroll=16)
    flushed(2, ov0, 0).start()

    for d in (1, 2, 3):
        for copy in exchange(d):
            copy.wait_send()
    flushed(0, ov2, 256).wait()
    flushed(1, ov1, 128).wait()
    flushed(2, ov0, 0).wait()
    for d in range(4):

        @pl.when(has_next)
        def _():
            for copy in first(d):
                copy.wait_send()

        @pl.when(passes)
        def _():
            for copy in second(d):
                copy.wait_send()


def place(a, b, held, came, went):
    size = a.shape[0] // PARTS

    def part(ref, i):
        return ref.at[pl.ds(i * size, size)]

    come = [pltpu.make_async_copy(part(a, i), part(held, i), came.at[i]) for i in range(PARTS)]
    go = [pltpu.make_async_copy(part(held, i), part(b, i), went.at[i]) for i in range(PARTS)]
    for copy in come:
        copy.start()
    for i in range(PARTS):
        come[i].wait()
        go[i].start()
    for copy in go:
        copy.wait()


def per_device(n, queries, keys, values, lengths):
    hbm = pl.BlockSpec(memory_space=pltpu.HBM)
    sems = pltpu.SemaphoreType.DMA((4, 2))
    attended = pl.pallas_call(
        functools.partial(kernel, n),
        out_shape=jax.ShapeDtypeStruct(queries.shape, BF16),
        in_specs=[hbm] * 4,
        out_specs=hbm,
        scratch_shapes=[pltpu.VMEM((512, 2048), BF16)]
        + [pltpu.VMEM((512, 256), BF16)] * 2
        + [pltpu.VMEM((256, 256), BF16)] * 6
        + [pltpu.VMEM((128, 256), BF16)] * 4
        + [pltpu.VMEM((512, 512), F32)]
        + [pltpu.VMEM((512, 256), F32)] * 3
        + [pltpu.VMEM((256, 128), F32), pltpu.VMEM((128, 128), F32)]
        + [
            pltpu.VMEM((16, 512, 256), F32),
            pltpu.VMEM((16, 512, 128), F32),
            pltpu.VMEM((2, 512, 512), F32),
            pltpu.SMEM((64,), jnp.int32),
            pltpu.SemaphoreType.DMA((4,)),
        ]
        + [sems] * 6
        + [pltpu.SemaphoreType.DMA((3,)), pltpu.VMEM((256, 2048), BF16)]
        + [pltpu.VMEM((128, 2048), BF16)] * 2,
        compiler_params=pltpu.CompilerParams(
            collective_id=0, has_side_effects=True, vmem_limit_bytes=58 * 2**20
        ),
    )(queries, keys, values, lengths)
    return pl.pallas_call(
        place,
        out_shape=jax.ShapeDtypeStruct(queries.shape, BF16),
        in_specs=[hbm],
        out_specs=hbm,
        scratch_shapes=[pltpu.VMEM(queries.shape, BF16)] + [pltpu.SemaphoreType.DMA((PARTS,))] * 2,
    )(attended)


def solution(mesh):
    placed = (P("ctx", "head"), P(("ctx", "head"), None), P(("ctx", "head"), None), P())
    return jax.shard_map(
        functools.partial(per_device, mesh.shape["ctx"]),
        mesh=mesh,
        in_specs=placed,
        out_specs=P("ctx", "head"),
        check_vma=False,
    )
```

time: 45.3 us -> 40 us (0.88)
  the two profiles are of different devices: /device:TPU:16 before, /device:TPU:25 now
where the time goes in v2:
time: 40 us; the launch traced here: 39.9 us
  Pallas kernels  39.9 us (100%)
    pallas_call x1, Pallas kernels, per_device(): pl.pallas_call(functools.partial(kernel, n), out_shape=jax.ShapeDtypeStru...  37.4 us
    pallas_call x1, Pallas kernels, per_device(): pl.pallas_call(place, out_shape=jax.ShapeDtypeStruct(queries.shape, BF16)...  2.42 us

profile of v2, /device:TPU:25, one launch (start us, length us, event | category | flops | bytes accessed | tf_op | source)
XLA Modules:
  0.0 39.9 jit_solution(11948949576219678572)
XLA Ops:
  0.0 37.4 %shard_map.46.a = bf16[512,2048]{1,0:T(8,128)(2,1)} custom-call(bf16[512,2048]{1,0:T(8,128)(2,1)} %q_hbm.1, bf16[128,1024]{1,0:T(8,128)(2,1)} %k_hbm.1, bf16[128,1024]{1,0:T(8,128)(2,1)} %v_hbm.1, s32[64]{0:T(128)} %len_hbm.1), custom_call_target="tpu_custom_call" | custom-call | tf_op jit(solution)/shard_map/pallas_call | solution.py:328
  37.4 2.4 %shard_map.47 = bf16[512,2048]{1,0:T(8,128)(2,1)} custom-call(bf16[512,2048]{1,0:T(8,128)(2,1)} %shard_map.46.a), custom_call_target="tpu_custom_call" | custom-call | tf_op jit(solution)/shard_map/pallas_call | solution.py:354

commit v3 on v2

--- a/solution.py
+++ b/solution.py
@@ -21,8 +21,8 @@
 
 
 def kernel(
-    n, q_hbm, k_hbm, v_hbm, len_hbm, out, qv, ko, vo, k1a, v1a, k1b, v1b, k2h, v2h, k21, v21, k20, v20,
-    bo, b1a, b1b, b2h, b21, b20, acc, top, sb, lens, loc, a_send, a_recv, s1, r1, s2, r2, flush, ov2, ov1, ov0,
+    n, q_hbm, k_hbm, v_hbm, len_hbm, out, qv, ko, vo, k1a, v1a, k1b, v1b, k2p, v2p, k2q, v2q, k21, v21, k20, v20,
+    bo, b1a, b1b, b2p, b2q, b21, b20, acc, top, sb, lens, loc, a_send, a_recv, s1, r1, s2, r2, flush, ov2, ov1, ov0,
 ):
     c = lax.axis_index("ctx")
     h = lax.axis_index("head")
@@ -42,6 +42,7 @@
     src, own = (k_hbm, v_hbm), (ko, vo)
     one = ((k1a, v1a), (k1a, v1a), (k1b, v1b), (k1b, v1b))
     low = ((k20, v20), (k21, v21))
+    high = ((k2p, v2p), (k2q, v2q))
 
     def remote(a, b, send, recv, device):
         return pltpu.make_async_remote_copy(
@@ -66,7 +67,7 @@
     def second(d, b=None):
         return [
             remote(
-                one[d][t].at[rows(hx[d] % 2)], (k2h, v2h)[t].at[rows(hx[d] % 2)] if b is None else low[b][t],
+                one[d][t].at[rows(hx[d] % 2)], high[d % 2][t] if b is None else low[b][t],
                 s2.at[d, t], r2.at[d, t], (c + 1, h),
             )
             for t in (0, 1)
@@ -115,7 +116,7 @@
 
     @pl.when(c <= 1)
     def _():
-        for ref in (k2h, v2h, k21, v21, k20, v20):
+        for ref in (k2p, v2p, k2q, v2q, k21, v21, k20, v20):
             ref[...] = jnp.zeros(ref.shape, BF16)
 
     local[0].wait()
@@ -139,7 +140,7 @@
             pos = tok + r + lax.broadcasted_iota(jnp.int32, (128, 128), 0)
             for ref, base, size in (
                 (bo, tok, 512), (b1a, tok - 512 + 256 * hh, 256), (b1b, tok - 256 - 256 * hh, 256),
-                (b2h, tok - 768, 256), (b21, tok - 896, 128), (b20, tok - 1024, 128),
+                (b2p, tok - 768 + 128 * (h % 2), 128), (b2q, tok - 640 - 128 * (h % 2), 128), (b21, tok - 896, 128), (b20, tok - 1024, 128),
             ):
                 if (ref is b21 and r >= 256) or (ref is b20 and r >= 128):
                     continue
@@ -187,13 +188,15 @@
                 o = dot(p, v, 1, 0)
                 if not opening:
                     o = acc[head, r : r + nr, :] * jnp.tile(jnp.exp2(old - new), (1, 2)) + o
+                keep = nr
                 if closing is not None:
-                    closing[:, pl.ds(pl.multiple_of(head * HD, HD), HD)] = (
-                        o[:, 0:HD] / o[:, HD : 2 * HD]
+                    ref, keep = closing
+                    ref[:, pl.ds(pl.multiple_of(head * HD, HD), HD)] = (
+                        o[keep:, 0:HD] / o[keep:, HD : 2 * HD]
                     ).astype(BF16)
-                else:
-                    acc[head, r : r + nr, :] = o
-                    top[head, r : r + nr, :] = new
+                if keep:
+                    acc[head, r : r + keep, :] = o[:keep]
+                    top[head, r : r + keep, :] = new[:keep]
 
         scores(0, 0)
 
@@ -241,28 +244,27 @@
         forward(cond, 0, (3, 1, 0))
         forward(cond, 1, (2, 3))
 
-    stage(ko, vo, bo, [(0, 256, 0, 256, None), (256, 256, 0, 512, None)], True)
-
-    @pl.when(has_prev)
-    def _():
-        taken(first(0))
-        taken(first(1))
-
-    forward_early(z != 0)
-
-    def middle():
-        forward_late(z != 0)
-        forward_early(z == 0)
-
-    stage(k1a, v1a, b1a, [(0, 512, 0, 256, None)], between=middle)
+    def take_first(cond):
+        @pl.when(has_prev & cond)
+        def _():
+            taken(first(0))
+            taken(first(1))
+
+    def early():
+        take_first(z != 0)
+        forward_early(z != 0)
+
+    stage(ko, vo, bo, [(0, 256, 0, 256, None), (256, 256, 0, 512, None)], True, early)
+    take_first(z == 0)
+    forward_late(z != 0)
+    stage(k1a, v1a, b1a, [(0, 512, 0, 256, None)], between=lambda: forward_early(z == 0))
     forward_late(z == 0)
     stage(k1b, v1b, b1b, [(0, 512, 0, 256, None)])
 
-    def landed(half, pieces):
+    def landed(half, d):
         @pl.when((c > 1) & (hh == half))
         def _():
-            for d in pieces:
-                taken(second(d))
+            taken(second(d))
 
     def landed_low(b):
         for half in (0, 1):
@@ -275,15 +277,18 @@
     def flushed(i, ref, r):
         return pltpu.make_async_copy(ref, out.at[r : r + ref.shape[0]], flush.at[i])
 
-    landed(0, (2, 3))
-    landed(1, (0, 1))
-    stage(k2h, v2h, b2h, [(0, 256, 0, 256, None), (256, 256, 0, 256, ov2)])
+    landed(0, 2)
+    landed(1, 0)
+    stage(k2p, v2p, b2p, [(0, 512, 0, 128, None)])
+    landed(0, 3)
+    landed(1, 1)
+    stage(k2q, v2q, b2q, [(0, 512, 0, 128, (ov2, 256))])
     flushed(0, ov2, 256).start()
     landed_low(1)
-    stage(k21, v21, b21, [(0, 128, 0, 128, None), (128, 128, 0, 128, ov1)], unroll=16)
+    stage(k21, v21, b21, [(0, 256, 0, 128, (ov1, 128))], unroll=16)
     flushed(1, ov1, 128).start()
     landed_low(0)
-    stage(k20, v20, b20, [(0, 128, 0, 128, ov0)], unroll=16)
+    stage(k20, v20, b20, [(0, 128, 0, 128, (ov0, 0))], unroll=16)
     flushed(2, ov0, 0).start()
 
     for d in (1, 2, 3):
@@ -332,10 +337,11 @@
         out_specs=hbm,
         scratch_shapes=[pltpu.VMEM((512, 2048), BF16)]
         + [pltpu.VMEM((512, 256), BF16)] * 2
-        + [pltpu.VMEM((256, 256), BF16)] * 6
-        + [pltpu.VMEM((128, 256), BF16)] * 4
+        + [pltpu.VMEM((256, 256), BF16)] * 4
+        + [pltpu.VMEM((128, 256), BF16)] * 8
         + [pltpu.VMEM((512, 512), F32)]
-        + [pltpu.VMEM((512, 256), F32)] * 3
+        + [pltpu.VMEM((512, 256), F32)] * 2
+        + [pltpu.VMEM((512, 128), F32)] * 2
         + [pltpu.VMEM((256, 128), F32), pltpu.VMEM((128, 128), F32)]
         + [
             pltpu.VMEM((16, 512, 256), F32),
@@ -351,13 +357,7 @@
             collective_id=0, has_side_effects=True, vmem_limit_bytes=58 * 2**20
         ),
     )(queries, keys, values, lengths)
-    return pl.pallas_call(
-        place,
-        out_shape=jax.ShapeDtypeStruct(queries.shape, BF16),
-        in_specs=[hbm],
-        out_specs=hbm,
-        scratch_shapes=[pltpu.VMEM(queries.shape, BF16)] + [pltpu.SemaphoreType.DMA((PARTS,))] * 2,
-    )(attended)
+    return jnp.where(lengths[0] > 0, attended, jnp.zeros_like(attended))
 
 
 def solution(mesh):

time: 40 us -> 40.2 us (level)
  the two profiles are of different devices: /device:TPU:25 before, /device:TPU:16 now
where the time goes in v3:
time: 40.2 us; the launch traced here: 40.1 us
  Pallas kernels  36.3 us (90%)
  other arithmetic  3.06 us (8%)
  between operations  0.66 us (2%)
    pallas_call x1, Pallas kernels, per_device(): pl.pallas_call(functools.partial(kernel, n), out_shape=jax.ShapeDtypeStru...  36.3 us
    select_n x1, other arithmetic, per_device(): return jnp.where(lengths[0] > 0, attended, jnp.zeros_like(attended))  3.06 us

profile of v3, /device:TPU:16, one launch (start us, length us, event | category | flops | bytes accessed | tf_op | source)
XLA Modules:
  0.0 40.1 jit_solution(16578348650201654862)
XLA Ops:
  0.7 36.3 %shard_map.46 = bf16[512,2048]{1,0:T(8,128)(2,1)} custom-call(bf16[512,2048]{1,0:T(8,128)(2,1)} %q_hbm.1, bf16[128,1024]{1,0:T(8,128)(2,1)} %k_hbm.1, bf16[128,1024]{1,0:T(8,128)(2,1)} %v_hbm.1, s32[64]{0:T(128)} %len_hbm.1), custom_call_target="tpu_custom_call" | custom-call | tf_op jit(solution)/shard_map/pallas_call | solution.py:333
  37.0 3.1 %broadcast_select_fusion = bf16[512,2048]{1,0:T(8,128)(2,1)} fusion(bf16[512,2048]{1,0:T(8,128)(2,1)} %shard_map.46, pred[]{:T(512)} %bitcast), kind=kLoop, calls=%fused_computation | loop fusion | flops 1048576 | bytes 4194305 | tf_op jit(solution)/shard_map/jit(_where)/select_n | solution.py:360

commit v4 on v3

--- a/solution.py
+++ b/solution.py
@@ -287,22 +287,24 @@
     landed_low(1)
     stage(k21, v21, b21, [(0, 256, 0, 128, (ov1, 128))], unroll=16)
     flushed(1, ov1, 128).start()
+    for d in (1, 2, 3):
+        for copy in exchange(d):
+            copy.wait_send()
+    for d in range(4):
+
+        @pl.when(has_next)
+        def _():
+            for copy in first(d):
+                copy.wait_send()
+
+    flushed(0, ov2, 256).wait()
     landed_low(0)
     stage(k20, v20, b20, [(0, 128, 0, 128, (ov0, 0))], unroll=16)
     flushed(2, ov0, 0).start()
 
-    for d in (1, 2, 3):
-        for copy in exchange(d):
-            copy.wait_send()
-    flushed(0, ov2, 256).wait()
     flushed(1, ov1, 128).wait()
     flushed(2, ov0, 0).wait()
     for d in range(4):
-
-        @pl.when(has_next)
-        def _():
-            for copy in first(d):
-                copy.wait_send()
 
         @pl.when(passes)
         def _():
@@ -357,7 +359,13 @@
             collective_id=0, has_side_effects=True, vmem_limit_bytes=58 * 2**20
         ),
     )(queries, keys, values, lengths)
-    return jnp.where(lengths[0] > 0, attended, jnp.zeros_like(attended))
+    return pl.pallas_call(
+        place,
+        out_shape=jax.ShapeDtypeStruct(queries.shape, BF16),
+        in_specs=[hbm],
+        out_specs=hbm,
+        scratch_shapes=[pltpu.VMEM(queries.shape, BF16)] + [pltpu.SemaphoreType.DMA((PARTS,))] * 2,
+    )(attended)
 
 
 def solution(mesh):

time: 40.2 us -> 38.7 us (0.963)
  other arithmetic: 3.06 us -> 0 us
  Pallas kernels: 36.3 us -> 38.6 us
  between operations: 0.66 us -> 0.01 us
    select_n x1 -> x0, other arithmetic: 3.06 us -> none  [per_device(): return jnp.where(lengths[0] > 0, attended, jnp.zeros_like(attended))]
    pallas_call x0 -> x1, Pallas kernels: none -> 2.42 us  [per_device(): pl.pallas_call(place, out_shape=jax.ShapeDtypeStruct(queries.shape, BF16)...]
where the time goes in v4:
time: 38.7 us; the launch traced here: 38.6 us
  Pallas kernels  38.6 us (100%)
    pallas_call x1, Pallas kernels, per_device(): pl.pallas_call(functools.partial(kernel, n), out_shape=jax.ShapeDtypeStru...  36.2 us
    pallas_call x1, Pallas kernels, per_device(): pl.pallas_call(place, out_shape=jax.ShapeDtypeStruct(queries.shape, BF16)...  2.42 us

profile of v4, /device:TPU:16, one launch (start us, length us, event | category | flops | bytes accessed | tf_op | source)
XLA Modules:
  0.0 38.6 jit_solution(12392579605761315428)
XLA Ops:
  0.0 36.2 %shard_map.46.a = bf16[512,2048]{1,0:T(8,128)(2,1)} custom-call(bf16[512,2048]{1,0:T(8,128)(2,1)} %q_hbm.1, bf16[128,1024]{1,0:T(8,128)(2,1)} %k_hbm.1, bf16[128,1024]{1,0:T(8,128)(2,1)} %v_hbm.1, s32[64]{0:T(128)} %len_hbm.1), custom_call_target="tpu_custom_call" | custom-call | tf_op jit(solution)/shard_map/pallas_call | solution.py:335
  36.2 2.4 %shard_map.47 = bf16[512,2048]{1,0:T(8,128)(2,1)} custom-call(bf16[512,2048]{1,0:T(8,128)(2,1)} %shard_map.46.a), custom_call_target="tpu_custom_call" | custom-call | tf_op jit(solution)/shard_map/pallas_call | solution.py:362

commit v5 on v4

--- a/solution.py
+++ b/solution.py
@@ -86,12 +86,12 @@
     def greet(device):
         pl.semaphore_signal(barrier, 1, device_id=device, device_id_type=MESH)
 
-    for d in (1, 2, 3):
-        greet((c, hx[d]))
-
     @pl.when(has_prev)
     def _():
         greet((c - 1, h))
+
+    for d in (1, 2, 3):
+        greet((c, hx[d]))
 
     local = [
         pltpu.make_async_copy(len_hbm, lens, loc.at[0]),
@@ -100,25 +100,6 @@
         pltpu.make_async_copy(q_hbm, qv, loc.at[3]),
     ]
     start(local)
-    pl.semaphore_wait(barrier, 3 + jnp.where(has_next, 1, 0))
-
-    @pl.when(has_next)
-    def _():
-        start(first(0))
-
-    for d in (1, 2, 3):
-        start(exchange(d))
-
-    @pl.when(c == 0)
-    def _():
-        for ref in (k1a, v1a, k1b, v1b):
-            ref[...] = jnp.zeros((256, 256), BF16)
-
-    @pl.when(c <= 1)
-    def _():
-        for ref in (k2p, v2p, k2q, v2q, k21, v21, k20, v20):
-            ref[...] = jnp.zeros(ref.shape, BF16)
-
     local[0].wait()
     tok = c * 512
 
@@ -132,6 +113,25 @@
     lanes = tok + lax.broadcasted_iota(jnp.int32, (8, 512), 1)
     _, begin = lax.fori_loop(0, 8, later, (jnp.int32(0), jnp.zeros((8, 512), jnp.int32)))
     begin = begin.astype(F32)
+
+    pl.semaphore_wait(barrier, 3 + jnp.where(has_next, 1, 0))
+
+    @pl.when(has_next)
+    def _():
+        start(first(0))
+
+    for d in (1, 2, 3):
+        start(exchange(d))
+
+    @pl.when(c == 0)
+    def _():
+        for ref in (k1a, v1a, k1b, v1b):
+            ref[...] = jnp.zeros((256, 256), BF16)
+
+    @pl.when(c <= 1)
+    def _():
+        for ref in (k2p, v2p, k2q, v2q, k21, v21, k20, v20):
+            ref[...] = jnp.zeros(ref.shape, BF16)
 
     def masks():
         spread = lax.broadcasted_iota(jnp.int32, (128, 128), 1)

time: 38.7 us -> 38.7 us (level)
  no operation moved by 1% of the time
where the time goes in v5:
time: 38.7 us; the launch traced here: 38.6 us
  Pallas kernels  38.6 us (100%)
    pallas_call x1, Pallas kernels, per_device(): pl.pallas_call(functools.partial(kernel, n), out_shape=jax.ShapeDtypeStru...  36.2 us
    pallas_call x1, Pallas kernels, per_device(): pl.pallas_call(place, out_shape=jax.ShapeDtypeStruct(queries.shape, BF16)...  2.42 us

profile of v5, /device:TPU:16, one launch (start us, length us, event | category | flops | bytes accessed | tf_op | source)
XLA Modules:
  0.0 38.6 jit_solution(14340833349312458304)
XLA Ops:
  0.0 36.2 %shard_map.46.a = bf16[512,2048]{1,0:T(8,128)(2,1)} custom-call(bf16[512,2048]{1,0:T(8,128)(2,1)} %q_hbm.1, bf16[128,1024]{1,0:T(8,128)(2,1)} %k_hbm.1, bf16[128,1024]{1,0:T(8,128)(2,1)} %v_hbm.1, s32[64]{0:T(128)} %len_hbm.1), custom_call_target="tpu_custom_call" | custom-call | tf_op jit(solution)/shard_map/pallas_call | solution.py:335
  36.2 2.4 %shard_map.47 = bf16[512,2048]{1,0:T(8,128)(2,1)} custom-call(bf16[512,2048]{1,0:T(8,128)(2,1)} %shard_map.46.a), custom_call_target="tpu_custom_call" | custom-call | tf_op jit(solution)/shard_map/pallas_call | solution.py:362
